TPU v7x, 32 devices: a whole 2x2x4 slice. The times are simulated.
32 devices in a mesh: shot: 4 (over x, core), cmp: 8 (over z, y).
Axes of the slice: x: 2, y: 2, z: 4, core: 2. Of those that a mesh axis runs over, the one named last changes fastest.
Arguments:
- traces: float32 [4096, 1920], P(('shot', 'cmp')), may hold values from -6 to 6
- statics: int32 [4096], P(('shot', 'cmp')), may hold values from -24 to 24
- cmp_owner: int32 [4096, 1], P(('shot', 'cmp')), may hold values from 0 to 31; in each aligned block of 128 rows (0 to 127, 128 to 255, ...) at most 8 rows name the same one
- cmp_offset: int32 [4096], P(('shot', 'cmp')), may hold values from 0 to 31
- shot_id: int32 [4096], P(('shot', 'cmp')), may hold values from 0 to 511, as said below
- receiver_id: int32 [4096], P(('shot', 'cmp')), may hold values from 0 to 511
Outputs:
- source_corr: float32 [512, 128], P(('shot', 'cmp'))
- receiver_corr: float32 [512, 128], P(('shot', 'cmp'))
Inputs may be any that keep to these rules, and one draw needn't show every extreme that they name: `cmp_owner`: in the 128 traces of one device (aligned blocks of the trace dimension), no owner is named by more than 8 traces. `shot_id`: the traces of block k of 128 traces come from shots k * 16 to (k + 1) * 16 - 1.
All inputs are finite; a program needn't handle non-finite values.
Results may differ from a plain program's by a relative error of at most 0.000078.
Values sent between devices are 32-bit elements; how exact they have to be, the bound alone decides.
A program may use at most 128 MiB of HBM per device.

v0:
```python
import jax
import jax.numpy as jnp
from jax import lax
from jax.sharding import PartitionSpec as P

LAGS = 128
MAX_SHIFT = 24
CMP_DEV = 32
SHOT_DEV = 16
REC_DEV = 16


stack_scale = 0.125
highest = lax.Precision.HIGHEST


def shift_traces(traces, statics):
    sample_total = traces.shape[1]
    padded = jnp.pad(traces, ((0, 0), (MAX_SHIFT, 128 - MAX_SHIFT)))
    amount = statics + MAX_SHIFT
    step_bits = (2 * MAX_SHIFT).bit_length()
    for bit in range(step_bits):
        stride = 1 << bit
        moved = jnp.pad(padded[:, :-stride], ((0, 0), (stride, 0)))
        chosen = amount >> bit & 1 == 1
        padded = jnp.where(chosen[:, None], moved, padded)
    return padded[:, 2 * MAX_SHIFT : 2 * MAX_SHIFT + sample_total]


def correlate_bins(arrived, pilots, in_bin, sample_total):
    padded = jnp.pad(pilots, ((0, 0), (LAGS // 2, LAGS // 2)))
    hankel = jnp.stack([padded[:, lag : lag + sample_total] for lag in range(LAGS)], axis=1)
    hankel = hankel.reshape(CMP_DEV * LAGS, sample_total)
    scores = lax.dot_general(
        arrived,
        hankel,
        (((1,), (1,)), ((), ())),
        precision=highest,
        preferred_element_type=jnp.float32,
    )
    scores = scores.reshape(arrived.shape[0], CMP_DEV, LAGS)
    return jnp.einsum("rb,rbl->rl", in_bin, scores, precision=highest)


def local(traces, statics, cmp_owner, cmp_offset, shot_id, receiver_id):
    trace_total, sample_total = traces.shape
    devices = lax.axis_size(("shot", "cmp"))
    capacity = 2 * trace_total // devices
    slot_total = devices * capacity
    shifted = shift_traces(traces, statics)
    owners = cmp_owner[:, 0]
    member = (owners[:, None] == jnp.arange(devices, dtype=jnp.int32)[None, :]).astype(jnp.int32)
    ranks = jnp.sum(jnp.cumsum(member, axis=0) * member, axis=1) - 1
    target = owners * capacity + ranks
    outbox = jnp.zeros((slot_total, sample_total), jnp.float32).at[target].set(shifted)
    label_rows = (cmp_offset + 1)[:, None]
    labels = jnp.zeros((slot_total, label_rows.shape[1]), jnp.int32).at[target].set(label_rows)
    arrived, tags = (
        lax.all_to_all(outbox, ("shot", "cmp"), split_axis=0, concat_axis=0, tiled=True),
        lax.all_to_all(labels, ("shot", "cmp"), split_axis=0, concat_axis=0, tiled=True),
    )
    bins = tags[:, 0] - 1
    in_bin = (bins[:, None] == jnp.arange(CMP_DEV, dtype=jnp.int32)[None, :]).astype(jnp.float32)
    pilots = lax.dot_general(
        in_bin,
        arrived,
        (((0,), (0,)), ((), ())),
        precision=highest,
        preferred_element_type=jnp.float32,
    )
    lagged = correlate_bins(arrived, pilots, in_bin, sample_total) / sample_total
    returned = lax.all_to_all(lagged, ("shot", "cmp"), split_axis=0, concat_axis=0, tiled=True)
    per_trace = returned[target]
    own_shots = (
        (shot_id % SHOT_DEV)[None, :] == jnp.arange(SHOT_DEV, dtype=jnp.int32)[:, None]
    ).astype(jnp.float32)
    source_corr = (
        jnp.dot(own_shots, per_trace, precision=highest, preferred_element_type=jnp.float32)
        * stack_scale
    )
    wanted = jnp.arange(REC_DEV * lax.axis_size(("shot", "cmp")), dtype=jnp.int32)
    picked = (receiver_id[None, :] == wanted[:, None]).astype(jnp.float32)
    receiver_corr = lax.psum_scatter(
        jnp.dot(picked, per_trace, precision=highest, preferred_element_type=jnp.float32)
        * stack_scale,
        ("shot", "cmp"),
        scatter_dimension=0,
        tiled=True,
    )
    return (source_corr, receiver_corr)


def solution(mesh):
    return jax.shard_map(
        local,
        mesh=mesh,
        in_specs=(
            P(("shot", "cmp"), None),
            P(("shot", "cmp")),
            P(("shot", "cmp"), None),
            P(("shot", "cmp")),
            P(("shot", "cmp")),
            P(("shot", "cmp")),
        ),
        out_specs=(P(("shot", "cmp"), None), P(("shot", "cmp"), None)),
        check_vma=False,
    )
```

profile of v0, /device:TPU:0, one launch (start us, length us, event | category | flops | bytes accessed | tf_op | source)
XLA Modules:
  0.0 383.1 jit_solution(4177577031169130129)
XLA Ops:
  10.2 1.0 scatter_custom_fusion
  11.9 7.3 %all-to-all-start = ((s32[32,8,1]{1,2,0:T(1,128)}), s32[32,8,1]{1,2,0:T(1,128)S(1)}, u32[]{:S(2)}, u32[]{:S(2)}) async-start(s32[32,8,1]{1,2,0:T(1,128)} %bitcast.3), calls=%async_computation | async-start | bytes 32768 | tf_op jit(solution)/shard_map/all_to_all | solution.py:60
  19.9 1.5 pad_slice_fusion
  21.4 1.8 pad_select_fusion.4
  24.7 3.1 scatter_custom_fusion.1
  27.8 6.0 %all-to-all-start.1 = ((f32[32,8,1920]{2,1,0:T(8,128)}), f32[32,8,1920]{2,1,0:T(8,128)S(1)}, u32[]{:S(2)}, u32[]{:S(2)}) async-start(f32[32,8,1920]{2,1,0:T(8,128)} %bitcast.291), calls=%async_computation.1 | async-start | bytes 3932160 | tf_op jit(solution)/shard_map/all_to_all | solution.py:59
  34.1 46.8 %all-to-all-done.1 = f32[32,8,1920]{2,1,0:T(8,128)S(1)} async-done(((f32[32,8,1920]{2,1,0:T(8,128)}), f32[32,8,1920]{2,1,0:T(8,128)S(1)}, u32[]{:S(2)}, u32[]{:S(2)}) %all-to-all-start.1) | async-done | bytes 1966112 | tf_op jit(solution)/shard_map/all_to_all | solution.py:59
  80.9 0.9 fusion.5
  85.9 0.8 constant_dynamic-update-slice_fusion.122
  91.7 0.8 constant_dynamic-update-slice_fusion.115
  95.0 0.8 constant_dynamic-update-slice_fusion.111
  97.5 0.8 constant_dynamic-update-slice_fusion.108
  98.3 0.8 constant_dynamic-update-slice_fusion.107
  99.9 0.9 constant_dynamic-update-slice_fusion.105
  104.9 0.8 constant_dynamic-update-slice_fusion.99
  105.8 0.9 constant_dynamic-update-slice_fusion.98
  109.9 0.8 constant_dynamic-update-slice_fusion.93
  110.8 0.8 constant_dynamic-update-slice_fusion.92
  111.6 0.8 constant_dynamic-update-slice_fusion.91
  112.4 0.9 constant_dynamic-update-slice_fusion.90
  119.1 0.9 constant_dynamic-update-slice_fusion.82
  122.4 0.8 constant_dynamic-update-slice_fusion.78
  124.1 0.8 constant_dynamic-update-slice_fusion.76
  125.7 0.8 constant_dynamic-update-slice_fusion.74
  126.6 0.8 constant_dynamic-update-slice_fusion.73
  127.4 0.8 constant_dynamic-update-slice_fusion.72
  131.5 0.8 constant_dynamic-update-slice_fusion.67
  132.3 0.8 constant_dynamic-update-slice_fusion.66
  133.2 0.8 constant_dynamic-update-slice_fusion.65
  136.4 0.9 constant_dynamic-update-slice_fusion.61
  139.7 0.8 constant_dynamic-update-slice_fusion.57
  143.1 0.8 constant_dynamic-update-slice_fusion.53
  145.5 0.8 constant_dynamic-update-slice_fusion.50
  146.4 0.8 constant_dynamic-update-slice_fusion.49
  147.2 0.8 constant_dynamic-update-slice_fusion.48
  148.1 0.8 constant_dynamic-update-slice_fusion.47
  148.9 0.8 constant_dynamic-update-slice_fusion.46
  150.6 0.9 constant_dynamic-update-slice_fusion.44
  151.4 0.8 constant_dynamic-update-slice_fusion.43
  153.9 0.8 constant_dynamic-update-slice_fusion.40
  154.8 0.9 constant_dynamic-update-slice_fusion.39
  155.6 0.8 constant_dynamic-update-slice_fusion.38
  157.3 0.8 constant_dynamic-update-slice_fusion.36
  158.1 0.8 constant_dynamic-update-slice_fusion.35
  159.8 0.8 constant_dynamic-update-slice_fusion.33
  162.3 0.8 constant_dynamic-update-slice_fusion.30
  166.4 0.9 constant_dynamic-update-slice_fusion.25
  167.3 0.9 constant_dynamic-update-slice_fusion.24
  168.2 0.8 constant_dynamic-update-slice_fusion.23
  169.0 0.8 constant_dynamic-update-slice_fusion.22
  172.3 0.8 constant_dynamic-update-slice_fusion.18
  174.0 0.9 constant_dynamic-update-slice_fusion.16
  174.8 0.8 constant_dynamic-update-slice_fusion.15
  178.2 0.8 constant_dynamic-update-slice_fusion.11
  181.5 0.8 constant_dynamic-update-slice_fusion.7
  182.3 0.9 constant_dynamic-update-slice_fusion.6
  184.0 0.8 constant_dynamic-update-slice_fusion.4
  187.3 0.8 constant_dynamic-update-slice_fusion
  188.1 39.7 %fusion = f32[256,32,128]{2,0,1:T(8,128)S(1)} fusion(f32[32,128,1920]{2,0,1:T(8,128)} %constant_dynamic-update-slice_fusion, f32[32,8,1920]{2,1,0:T(8,128)S(1)} %all-to-all-done.1), kind=kOutput, calls=%fused_computation.3 | convolution fusion | flops 24159191040 | bytes 37617664 | tf_op jit(solution)/shard_map/dot_general | solution.py:34
  227.8 4.4 %fusion.2 = f32[256,1,128]{2,1,0:T(1,128)S(1)} fusion(f32[256,32,128]{2,0,1:T(8,128)S(1)} %fusion, pred[256,32,1]{1,0,2:T(32,128)(4,1)S(1)} %fusion.13), kind=kOutput, calls=%fused_computation.5 | convolution fusion | flops 12582912 | bytes 4333568 | tf_op jit(solution)/shard_map/rb,rbl->rl/dot_general | solution.py:42
  232.9 2.6 all-to-all-start.2
  235.5 7.7 %all-to-all-done.2 = f32[32,8,128]{2,1,0:T(8,128)S(1)} async-done(((f32[32,8,128]{2,1,0:T(8,128)}), f32[32,8,128]{2,1,0:T(8,128)S(1)}, u32[]{:S(2)}, u32[]{:S(2)}) %all-to-all-start.2) | async-done | bytes 131104 | tf_op jit(solution)/shard_map/all_to_all | solution.py:72
  243.9 1.0 convolution_multiply_fusion
  245.6 130.6 %reduce-scatter.2.cloned.1.call-done = f32[16,128]{1,0:T(8,128)} async-done(((f32[512,128]{1,0:T(8,128)}), f32[16,128]{1,0:T(8,128)}) %reduce-scatter.2.cloned.1.call-update) | async-done | bytes 8208 | tf_op jit(solution)/shard_map/reduce_scatter | solution.py:83
  (104 shorter events, 72.3 us)
Async XLA Ops:
  11.9 15.9 %all-to-all-start = ((s32[32,8,1]{1,2,0:T(1,128)}), s32[32,8,1]{1,2,0:T(1,128)S(1)}, u32[]{:S(2)}, u32[]{:S(2)}) async-start(s32[32,8,1]{1,2,0:T(1,128)} %bitcast.3), calls=%async_computation | async-start | bytes 32768 | tf_op jit(solution)/shard_map/all_to_all | solution.py:60
  27.8 53.1 %all-to-all-start.1 = ((f32[32,8,1920]{2,1,0:T(8,128)}), f32[32,8,1920]{2,1,0:T(8,128)S(1)}, u32[]{:S(2)}, u32[]{:S(2)}) async-start(f32[32,8,1920]{2,1,0:T(8,128)} %bitcast.291), calls=%async_computation.1 | async-start | bytes 3932160 | tf_op jit(solution)/shard_map/all_to_all | solution.py:59
  162.3 81.6 %copy-start = (s32[128]{0:T(128)S(1)}, s32[128]{0:T(128)}, u32[]{:S(2)}) copy-start(s32[128]{0:T(128)} %param.11) | copy-start | bytes 1540
  163.1 81.7 %copy-start.1 = (s32[128]{0:T(128)S(1)}, s32[128]{0:T(128)}, u32[]{:S(2)}) copy-start(s32[128]{0:T(128)} %param.10) | copy-start | bytes 1540
  232.9 10.3 %all-to-all-start.2 = ((f32[32,8,128]{2,1,0:T(8,128)}), f32[32,8,128]{2,1,0:T(8,128)S(1)}, u32[]{:S(2)}, u32[]{:S(2)}) async-start(f32[32,8,128]{2,1,0:T(8,128)} %multiply_bitcast_fusion), calls=%async_computation.2 | async-start | bytes 262144 | tf_op jit(solution)/shard_map/all_to_all | solution.py:72
  235.5 140.7 %reduce-scatter.2.cloned.1.call-start = ((), (), s32[]{:S(2)}) async-start(), calls=%async_computation.4 | async-start | bytes 270336 | tf_op jit(solution)/shard_map/reduce_scatter | solution.py:83
Sparse Core Ops, SparseCore 0:
  245.0 131.2 reduce-scatter.1
where the time goes:
time: 384 us; the launch traced here: 383 us
  waiting for transfers between devices  185 us (48%)
  local copies, waits for them, and re-layouts  110 us (29%)
  matrix products  46.7 us (12%)
  starting transfers between devices  15.9 us (4%)
  between operations  14.2 us (4%)
  other arithmetic  10.9 us (3%)
    reduce_scatter x1, waiting for transfers between devices, local(): lax.psum_scatter(jnp.dot(picked, per_trace, precision=highest, preferred_...  131 us
    unnamed x131, local copies, waits for them, and re-layouts  105 us
    all_to_all x1, waiting for transfers between devices, local(): lax.all_to_all(outbox, ('shot', 'cmp'), split_axis=0, concat_axis=0, tile...  46.8 us
    dot_general x1, matrix products, correlate_bins(): lax.dot_general(arrived, hankel, (((1,), (1,)), ((), ())), precision=high...  39.7 us
  transfers between devices with their start and end apart: 4, of which 3 were waited for; matrix products, arithmetic and copies ran while one was open for 3% of the time, Pallas kernels for 0%

commit v1 on v0

v1 whole, which is shorter than its diff:
```python
import functools

import jax
import jax.numpy as jnp
import ml_dtypes
import numpy as np
from jax import lax
from jax.experimental import pallas as pl
from jax.experimental.pallas import tpu as pltpu
from jax.sharding import PartitionSpec as P

LAGS = 128
MAX_SHIFT = 24
CMP_DEV = 32
SHOT_DEV = 16
REC_DEV = 16
BLOCK = 128
STACK_SCALE = 0.125

f32 = jnp.float32
bf16 = jnp.bfloat16
MESH = pl.DeviceIdType.MESH


def transform_tables(sample_total):
    u = np.arange(BLOCK)[:, None]
    f = np.arange(BLOCK)[None, :]
    angle = 2 * np.pi * ((u * f) % 256) / 256
    imag = -np.sin(angle)
    imag[:, 0] = 1 - 2 * (np.arange(BLOCK) % 2)
    forward = np.concatenate([np.cos(angle), imag], axis=1)
    weight = np.full((BLOCK, 1), 2.0)
    weight[0] = 1
    back_imag = -2 * np.sin(angle)
    back_imag[0] = 1 - 2 * (np.arange(BLOCK) % 2)
    inverse = np.concatenate([weight * np.cos(angle), back_imag], axis=0)
    inverse = inverse / 256 / sample_total * STACK_SCALE
    tables = []
    for table in (forward, inverse):
        high = table.astype(ml_dtypes.bfloat16)
        low = (table - high.astype(np.float64)).astype(ml_dtypes.bfloat16)
        tables += [high, low]
    return tables


def halves(x):
    high = x.astype(bf16)
    return high, (x - high.astype(f32)).astype(bf16)


def mm(a, b):
    return jnp.dot(a, b, preferred_element_type=f32)


def mm_nt(a, b):
    return lax.dot_general(a, b, (((1,), (1,)), ((), ())), preferred_element_type=f32)


def mm3(a, b_high, b_low):
    high, low = halves(a)
    return mm(high, b_high) + mm(low, b_high) + mm(high, b_low)


def iota(shape, dim):
    return lax.broadcasted_iota(jnp.int32, shape, dim)


def onehot(mask):
    return jnp.where(mask, 1.0, 0.0).astype(bf16)


def exact_dot(a, b):
    return jnp.dot(a, b, precision=lax.Precision.HIGHEST, preferred_element_type=f32)


def kernel(
    n, n_cmp, cap,
    owner_ref, offset_ref, shot_ref, receiver_ref, statics_ref, traces_ref,
    fwd_high_ref, fwd_low_ref, inv_high_ref, inv_low_ref,
    source_ref, received_ref,
    shifted, outbox, inbox, label_rows, label_out, label_in, spectra, corr, lag_out, lag_in, rec_out, rec_in,
    send_sem, recv_sem,
):
    rows = n * cap
    traces, samples = traces_ref.shape
    blocks = samples // BLOCK
    me = lax.axis_index("shot") * n_cmp + lax.axis_index("cmp")

    def place(d):
        return (d // n_cmp, lax.rem(d, n_cmp))

    barrier = pltpu.get_barrier_semaphore()

    @pl.loop(1, n)
    def _(k):
        pl.semaphore_signal(barrier, inc=1, device_id=place(lax.rem(me + k, n)), device_id_type=MESH)

    def trace_copy(d, slot):
        return pltpu.make_async_remote_copy(
            src_ref=outbox.at[pl.ds(pl.multiple_of(d * cap, 8), cap)],
            dst_ref=inbox.at[pl.ds(pl.multiple_of(slot * cap, 8), cap)],
            send_sem=send_sem.at[0, d], recv_sem=recv_sem.at[0, slot], device_id=place(d), device_id_type=MESH,
        )

    def label_copy(d, slot):
        return pltpu.make_async_remote_copy(
            src_ref=label_out.at[d], dst_ref=label_in.at[slot],
            send_sem=send_sem.at[1, d], recv_sem=recv_sem.at[1, slot], device_id=place(d), device_id_type=MESH,
        )

    def lag_copy(d, slot):
        return pltpu.make_async_remote_copy(
            src_ref=lag_out.at[pl.ds(pl.multiple_of(d * cap, 8), cap)],
            dst_ref=lag_in.at[pl.ds(pl.multiple_of(slot * cap, 8), cap)],
            send_sem=send_sem.at[2, d], recv_sem=recv_sem.at[2, slot], device_id=place(d), device_id_type=MESH,
        )

    def rec_copy(d, slot):
        return pltpu.make_async_remote_copy(
            src_ref=rec_out.at[pl.ds(pl.multiple_of(d * REC_DEV, 8), REC_DEV)],
            dst_ref=rec_in.at[pl.ds(pl.multiple_of(slot * REC_DEV, 8), REC_DEV)],
            send_sem=send_sem.at[3, d], recv_sem=recv_sem.at[3, slot], device_id=place(d), device_id_type=MESH,
        )

    statics_row = statics_ref[...]
    eye = iota((traces, traces), 0) == iota((traces, traces), 1)
    amount = jnp.sum(jnp.where(eye, statics_row, 0), axis=1, keepdims=True) + MAX_SHIFT
    step = 16
    for first in range(0, traces, step):
        row = jnp.concatenate([traces_ref[first : first + step, :], jnp.zeros((step, BLOCK), f32)], axis=1)
        width = samples + BLOCK
        here = amount[first : first + step]
        row = pltpu.roll(row, width - MAX_SHIFT, 1)
        for bit in range((2 * MAX_SHIFT).bit_length()):
            row = jnp.where((here >> bit) & 1 == 1, pltpu.roll(row, 1 << bit, 1), row)
        high, low = halves(row[:, :samples])
        shifted[first : first + step, :] = high
        shifted[traces + first : traces + first + step, :] = low

    owner = owner_ref[...]
    member = iota((n, traces), 0) == owner
    upper = onehot(iota((traces, traces), 0) <= iota((traces, traces), 1))
    counts = mm(onehot(member), upper)
    rank = jnp.sum(jnp.where(member, counts, 0.0), axis=0, keepdims=True).astype(jnp.int32) - 1
    target = owner * cap + rank
    put = onehot(iota((rows, traces), 0) == target)
    put_twice = jnp.concatenate([put, put], axis=1)
    for first in range(0, samples, 3 * BLOCK):
        outbox[:, first : first + 3 * BLOCK] = mm(put_twice, shifted[:, first : first + 3 * BLOCK])

    seat = iota((BLOCK, traces), 0)
    bins_here = jnp.where(member, (offset_ref[...] + 1).astype(f32), 0.0)
    rec_here = jnp.where(member, (receiver_ref[...] + 1).astype(f32), 0.0)

    def exact_nt(a, b):
        return lax.dot_general(
            a, b, (((1,), (1,)), ((), ())), precision=lax.Precision.HIGHEST, preferred_element_type=f32
        )

    label_rows[...] = exact_nt(bins_here, jnp.where(seat == rank, 1.0, 0.0)) + exact_nt(
        rec_here, jnp.where(seat == rank + 64, 1.0, 0.0)
    )

    @pl.loop(0, n)
    def _(d):
        label_out[d] = label_rows[pl.ds(d, 1), :]

    pl.semaphore_wait(barrier, n - 1)

    @pl.loop(1, n)
    def _(k):
        d = lax.rem(me + k, n)
        label_copy(d, me).start()
        trace_copy(d, me).start()

    mine = pl.ds(pl.multiple_of(me * cap, 8), cap)
    inbox[mine, :] = outbox[mine, :]
    label_in[me] = label_out[me]

    own_shot = onehot(iota((SHOT_DEV, traces), 0) == lax.rem(shot_ref[...], SHOT_DEV))
    take = mm_nt(own_shot, put).astype(bf16)

    @pl.loop(1, n)
    def _(k):
        d = lax.rem(me + (n - k), n)
        label_copy(d, d).wait_recv()
        trace_copy(d, d).wait_recv()

    @pl.loop(0, n)
    def _(d):
        label_rows[pl.ds(d, 1), :] = label_in[d]

    labels = label_rows[...]
    spread = jnp.where(iota((rows, n), 0) // cap == iota((rows, n), 1), 1.0, 0.0)
    slot_col = iota((rows, BLOCK), 0) % cap
    lane_col = iota((rows, BLOCK), 1)
    per_slot = exact_dot(spread, labels)
    bin_col = jnp.sum(jnp.where(slot_col == lane_col, per_slot, 0.0), axis=1, keepdims=True).astype(jnp.int32) - 1
    slot_row = iota((BLOCK, rows), 1) % cap
    lane_row = iota((BLOCK, rows), 0)
    mine_row = iota((n, rows), 1) // cap == iota((n, rows), 0)
    bin_all = exact_dot(labels, jnp.where(slot_row == lane_row, 1.0, 0.0))
    rec_all = exact_dot(labels, jnp.where(slot_row + 64 == lane_row, 1.0, 0.0))
    bin_row = jnp.sum(jnp.where(mine_row, bin_all, 0.0), axis=0, keepdims=True).astype(jnp.int32) - 1
    rec_row = jnp.sum(jnp.where(mine_row, rec_all, 0.0), axis=0, keepdims=True).astype(jnp.int32) - 1
    gather = onehot(iota((rows, CMP_DEV), 1) == bin_col)
    gather_twice = jnp.concatenate([gather, gather], axis=1)
    stack = onehot(iota((CMP_DEV, rows), 0) == bin_row)
    pick = onehot(iota((REC_DEV * n, rows), 0) == rec_row)

    pilots = []
    for j in range(blocks):
        high, low = halves(inbox[:, j * BLOCK : (j + 1) * BLOCK])
        pilots.append(mm(stack, high) + mm(stack, low))
    pilots.append(jnp.zeros((CMP_DEV, BLOCK), f32))
    moved = pltpu.roll(jnp.concatenate(pilots, axis=1), LAGS // 2, 1)
    fwd_high, fwd_low = fwd_high_ref[...], fwd_low_ref[...]
    for j in range(blocks + 1):
        spectra[j] = mm3(moved[:, j * BLOCK : (j + 1) * BLOCK], fwd_high, fwd_low)

    lane = iota((CMP_DEV, BLOCK), 1)
    turn = (1 - 2 * (iota((CMP_DEV, 2 * BLOCK), 1) % 2)).astype(f32)
    corr[...] = jnp.zeros_like(corr)

    @pl.loop(0, blocks)
    def _(j):
        window = spectra[j] + turn * spectra[j + 1]
        real, imag = window[:, :BLOCK], window[:, BLOCK:]
        wide = jnp.concatenate(
            [real, jnp.where(lane == 0, 0.0, imag), jnp.where(lane == 0, -imag, real)], axis=1
        )
        w = mm(gather_twice, jnp.concatenate(halves(wide), axis=0))
        y = mm3(inbox[:, pl.ds(pl.multiple_of(j * BLOCK, BLOCK), BLOCK)], fwd_high, fwd_low)
        y_real, y_imag = y[:, :BLOCK], y[:, BLOCK:]
        w_real, w_imag, w_other = w[:, :BLOCK], w[:, BLOCK : 2 * BLOCK], w[:, 2 * BLOCK :]
        corr[:, :BLOCK] += y_real * w_real + y_imag * w_imag
        corr[:, BLOCK:] += y_real * w_imag - y_imag * w_other

    lagged = mm3(corr[...], inv_high_ref[...], inv_low_ref[...])
    lag_out[...] = lagged
    high, low = halves(lagged)
    rec_out[...] = mm(pick, high) + mm(pick, low)

    @pl.loop(1, n)
    def _(k):
        d = lax.rem(me + k, n)
        rec_copy(d, me).start()
        lag_copy(d, me).start()

    lag_in[mine, :] = lag_out[mine, :]
    mine_rec = pl.ds(pl.multiple_of(me * REC_DEV, 8), REC_DEV)
    rec_in[mine_rec, :] = rec_out[mine_rec, :]

    @pl.loop(1, n)
    def _(k):
        d = lax.rem(me + (n - k), n)
        rec_copy(d, d).wait_recv()
        lag_copy(d, d).wait_recv()

    high, low = halves(lag_in[...])
    source_ref[...] = mm(take, high) + mm(take, low)
    total = rec_in[0:REC_DEV, :]
    for d in range(1, n):
        total = total + rec_in[d * REC_DEV : (d + 1) * REC_DEV, :]
    received_ref[...] = total

    @pl.loop(1, n)
    def _(k):
        d = lax.rem(me + k, n)
        label_copy(d, me).wait_send()
        trace_copy(d, me).wait_send()
        rec_copy(d, me).wait_send()
        lag_copy(d, me).wait_send()


def local(n, n_cmp, traces, statics, cmp_owner, cmp_offset, shot_id, receiver_id):
    count, samples = traces.shape
    cap = max(8, 2 * count // n)
    rows = n * cap

    def row(a):
        return a.reshape(1, count)

    tables = [jnp.asarray(t) for t in transform_tables(samples)]
    vmem = pl.BlockSpec(memory_space=pltpu.VMEM)
    return pl.pallas_call(
        functools.partial(kernel, n, n_cmp, cap),
        out_shape=(
            jax.ShapeDtypeStruct((SHOT_DEV, LAGS), f32),
            jax.ShapeDtypeStruct((REC_DEV, LAGS), f32),
        ),
        in_specs=[vmem] * 10,
        out_specs=(vmem, vmem),
        scratch_shapes=[
            pltpu.VMEM((2 * count, samples), bf16),
            pltpu.VMEM((rows, samples), f32),
            pltpu.VMEM((rows, samples), f32),
            pltpu.VMEM((n, BLOCK), f32),
            pltpu.VMEM((n, 1, BLOCK), f32),
            pltpu.VMEM((n, 1, BLOCK), f32),
            pltpu.VMEM((samples // BLOCK + 1, CMP_DEV, 2 * BLOCK), f32),
            pltpu.VMEM((rows, 2 * BLOCK), f32),
            pltpu.VMEM((rows, LAGS), f32),
            pltpu.VMEM((rows, LAGS), f32),
            pltpu.VMEM((n * REC_DEV, LAGS), f32),
            pltpu.VMEM((n * REC_DEV, LAGS), f32),
            pltpu.SemaphoreType.DMA((4, n)),
            pltpu.SemaphoreType.DMA((4, n)),
        ],
        compiler_params=pltpu.CompilerParams(
            collective_id=0, has_side_effects=True, vmem_limit_bytes=48 * 1024 * 1024
        ),
    )(row(cmp_owner), row(cmp_offset), row(shot_id), row(receiver_id), row(statics), traces, *tables)


def solution(mesh):
    axes = ("shot", "cmp")
    n = mesh.shape["shot"] * mesh.shape["cmp"]
    return jax.shard_map(
        functools.partial(local, n, mesh.shape["cmp"]),
        mesh=mesh,
        in_specs=(P(axes, None), P(axes), P(axes, None), P(axes), P(axes), P(axes)),
        out_specs=(P(axes, None), P(axes, None)),
        check_vma=False,
    )
```

time: 384 us -> 77.5 us (0.20)
  waiting for transfers between devices: 185 us -> 0 us
  local copies, waits for them, and re-layouts: 110 us -> 6.43 us
  Pallas kernels: 0 us -> 70.1 us
  matrix products: 46.7 us -> 0 us
  starting transfers between devices: 15.9 us -> 0 us
  between operations: 14.2 us -> 0.69 us
  other arithmetic: 10.9 us -> 0 us
    reduce_scatter x1 -> x0, waiting for transfers between devices: 131 us -> none  [local(): lax.psum_scatter(jnp.dot(picked, per_trace, precision=highest, preferred_...]
    unnamed x131 -> x22, local copies, waits for them, and re-layouts: 105 us -> 6.43 us
    pallas_call x0 -> x1, Pallas kernels: none -> 70.1 us  [local(): pl.pallas_call(functools.partial(kernel, n, n_cmp, cap), out_shape=(jax.S...]
    all_to_all x3 -> x0, waiting for transfers between devices: 54.5 us -> none  [the longest x1 46.8 us: local(): lax.all_to_all(outbox, ('shot', 'cmp'), split_axis=0, concat_axis=0, tile...]
    dot_general x5 -> x0, matrix products: 46.7 us -> none  [the longest x1 39.7 us: correlate_bins(): lax.dot_general(arrived, hankel, (((1,), (1,)), ((), ())), precision=high...]
    all_to_all x3 -> x0, starting transfers between devices: 15.9 us -> none  [the longest x1 7.3 us: local(): lax.all_to_all(labels, ('shot', 'cmp'), split_axis=0, concat_axis=0, tile...]
    select_n x7 -> x0, other arithmetic: 3.92 us -> none  [the longest x5 3.24 us: shift_traces(): padded = jnp.where(chosen[:, None], moved, padded)]
  transfers between devices with their start and end apart: 4 -> 0, of which waited for: 3 -> 0; matrix products, arithmetic and copies ran while one was open for 3% -> 0% of each run, Pallas kernels for 0% -> 0%
where the time goes in v1:
time: 77.5 us; the launch traced here: 77.2 us
  Pallas kernels  70.1 us (90%)
  local copies, waits for them, and re-layouts  6.43 us (8%)
    pallas_call x1, Pallas kernels, local(): pl.pallas_call(functools.partial(kernel, n, n_cmp, cap), out_shape=(jax.S...  70.1 us
    unnamed x22, local copies, waits for them, and re-layouts  6.43 us

profile of v1, /device:TPU:0, one launch (start us, length us, event | category | flops | bytes accessed | tf_op | source)
XLA Modules:
  0.0 77.2 jit_solution(9906794697107814447)
XLA Ops:
  0.6 0.0 copy-start.8
  0.6 0.0 copy-start.9
  0.7 0.0 copy-start.5
  0.7 0.0 copy-start.6
  0.7 0.0 copy-start.7
  0.7 0.6 copy-done.8
  1.3 0.0 copy-done.9
  1.3 0.0 copy-done.5
  1.3 0.0 copy-done.6
  1.3 0.0 copy-done.7
  1.4 0.0 copy-start
  1.4 1.2 %copy-done = f32[128,1920]{1,0:T(8,128)S(1)} copy-done((f32[128,1920]{1,0:T(8,128)S(1)}, f32[128,1920]{1,0:T(8,128)}, u32[]{:S(2)}) %copy-start) | copy-done | bytes 983064
  2.6 0.0 copy-start.1
  2.6 0.8 %copy-done.1 = bf16[256,128]{1,0:T(8,128)(2,1)S(1)} copy-done((bf16[256,128]{1,0:T(8,128)(2,1)S(1)}, bf16[256,128]{1,0:T(8,128)(2,1)}, u32[]{:S(2)}) %copy-start.1) | copy-done | bytes 65560
  3.4 0.0 copy-start.2
  3.4 0.8 %copy-done.2 = bf16[256,128]{1,0:T(8,128)(2,1)S(1)} copy-done((bf16[256,128]{1,0:T(8,128)(2,1)S(1)}, bf16[256,128]{1,0:T(8,128)(2,1)}, u32[]{:S(2)}) %copy-start.2) | copy-done | bytes 65560
  4.2 0.0 copy-start.3
  4.2 0.8 %copy-done.3 = bf16[128,256]{1,0:T(8,128)(2,1)S(1)} copy-done((bf16[128,256]{1,0:T(8,128)(2,1)S(1)}, bf16[128,256]{1,0:T(8,128)(2,1)}, u32[]{:S(2)}) %copy-start.3) | copy-done | bytes 65560
  5.1 0.0 copy-start.4
  5.1 0.8 %copy-done.4 = bf16[128,256]{1,0:T(8,128)(2,1)S(1)} copy-done((bf16[128,256]{1,0:T(8,128)(2,1)S(1)}, bf16[128,256]{1,0:T(8,128)(2,1)}, u32[]{:S(2)}) %copy-start.4) | copy-done | bytes 65560
  5.9 70.1 %shard_map.113 = (f32[16,128]{1,0:T(8,128)S(1)}, f32[16,128]{1,0:T(8,128)S(1)}) custom-call(s32[1,128]{1,0:T(1,128)S(1)} %bitcast.5, s32[1,128]{1,0:T(1,128)S(1)} %bitcast.6, s32[1,128]{1,0:T(1,128)S(1)} %bitcast.7, s32[1,128]{1,0:T(1,128)S(1)} %bitcast.8, s32[1,128]{1,0:T(1,128)S(1)} %bitcast.9, f32[128,1920]{1,0:T(8,128)S(1)} %copy-done, ...), custom_call_target="tpu_custom_call" | custom-call | tf_op jit(solution)/shard_map/pallas_call | solution.py:286
  76.0 0.6 copy.14
  76.6 0.6 copy.15
Async XLA Ops:
  0.6 0.7 copy-start.8
  0.6 0.7 copy-start.9
  0.7 0.7 copy-start.5
  0.7 0.7 copy-start.6
  0.7 0.7 copy-start.7
  1.4 1.2 %copy-start = (f32[128,1920]{1,0:T(8,128)S(1)}, f32[128,1920]{1,0:T(8,128)}, u32[]{:S(2)}) copy-start(f32[128,1920]{1,0:T(8,128)} %traces_ref.1) | copy-start | bytes 2949124
  2.6 0.8 %copy-start.1 = (bf16[256,128]{1,0:T(8,128)(2,1)S(1)}, bf16[256,128]{1,0:T(8,128)(2,1)}, u32[]{:S(2)}) copy-start(bf16[256,128]{1,0:T(8,128)(2,1)} %constant.11.clone.inv_low_ref) | copy-start | bytes 196612
  3.4 0.8 %copy-start.2 = (bf16[256,128]{1,0:T(8,128)(2,1)S(1)}, bf16[256,128]{1,0:T(8,128)(2,1)}, u32[]{:S(2)}) copy-start(bf16[256,128]{1,0:T(8,128)(2,1)} %constant.10.clone.inv_high_ref) | copy-start | bytes 196612
  4.2 0.8 %copy-start.3 = (bf16[128,256]{1,0:T(8,128)(2,1)S(1)}, bf16[128,256]{1,0:T(8,128)(2,1)}, u32[]{:S(2)}) copy-start(bf16[128,256]{1,0:T(8,128)(2,1)} %constant.9.clone.fwd_low_ref) | copy-start | bytes 196612
  5.1 0.8 %copy-start.4 = (bf16[128,256]{1,0:T(8,128)(2,1)S(1)}, bf16[128,256]{1,0:T(8,128)(2,1)}, u32[]{:S(2)}) copy-start(bf16[128,256]{1,0:T(8,128)(2,1)} %constant.8.clone.fwd_high_ref) | copy-start | bytes 196612

commit v2 on v1

--- a/solution.py
+++ b/solution.py
@@ -15,6 +15,7 @@
 SHOT_DEV = 16
 REC_DEV = 16
 BLOCK = 128
+PARTS = 3
 STACK_SCALE = 0.125
 
 f32 = jnp.float32
@@ -75,67 +76,80 @@
 
 def kernel(
     n, n_cmp, cap,
+    owner_any, offset_any, shot_any, receiver_any, statics_any, traces_any,
+    fwd_high_any, fwd_low_any, inv_high_any, inv_low_any,
+    source_ref, received_ref,
     owner_ref, offset_ref, shot_ref, receiver_ref, statics_ref, traces_ref,
     fwd_high_ref, fwd_low_ref, inv_high_ref, inv_low_ref,
-    source_ref, received_ref,
     shifted, outbox, inbox, label_rows, label_out, label_in, spectra, corr, lag_out, lag_in, rec_out, rec_in,
-    send_sem, recv_sem,
+    send_sem, recv_sem, load_sem,
 ):
     rows = n * cap
     traces, samples = traces_ref.shape
     blocks = samples // BLOCK
+    part = samples // PARTS
+    per_part = blocks // PARTS
     me = lax.axis_index("shot") * n_cmp + lax.axis_index("cmp")
 
     def place(d):
         return (d // n_cmp, lax.rem(d, n_cmp))
 
+    loads = [
+        pltpu.make_async_copy(here, there, load_sem.at[i])
+        for i, (here, there) in enumerate(
+            (
+                (owner_any, owner_ref),
+                (offset_any, offset_ref),
+                (shot_any, shot_ref),
+                (receiver_any, receiver_ref),
+                (statics_any, statics_ref),
+                (traces_any, traces_ref),
+                (fwd_high_any, fwd_high_ref),
+                (fwd_low_any, fwd_low_ref),
+                (inv_high_any, inv_high_ref),
+                (inv_low_any, inv_low_ref),
+            )
+        )
+    ]
+    for load in loads:
+        load.start()
+
     barrier = pltpu.get_barrier_semaphore()
 
     @pl.loop(1, n)
     def _(k):
         pl.semaphore_signal(barrier, inc=1, device_id=place(lax.rem(me + k, n)), device_id_type=MESH)
 
-    def trace_copy(d, slot):
+    def trace_copy(c, d, slot):
+        columns = pl.ds(c * part, part)
         return pltpu.make_async_remote_copy(
-            src_ref=outbox.at[pl.ds(pl.multiple_of(d * cap, 8), cap)],
-            dst_ref=inbox.at[pl.ds(pl.multiple_of(slot * cap, 8), cap)],
-            send_sem=send_sem.at[0, d], recv_sem=recv_sem.at[0, slot], device_id=place(d), device_id_type=MESH,
+            src_ref=outbox.at[pl.ds(pl.multiple_of(d * cap, 8), cap), columns],
+            dst_ref=inbox.at[pl.ds(pl.multiple_of(slot * cap, 8), cap), columns],
+            send_sem=send_sem.at[c, d], recv_sem=recv_sem.at[c, slot], device_id=place(d), device_id_type=MESH,
         )
 
     def label_copy(d, slot):
         return pltpu.make_async_remote_copy(
             src_ref=label_out.at[d], dst_ref=label_in.at[slot],
-            send_sem=send_sem.at[1, d], recv_sem=recv_sem.at[1, slot], device_id=place(d), device_id_type=MESH,
+            send_sem=send_sem.at[PARTS, d], recv_sem=recv_sem.at[PARTS, slot], device_id=place(d), device_id_type=MESH,
         )
 
     def lag_copy(d, slot):
         return pltpu.make_async_remote_copy(
             src_ref=lag_out.at[pl.ds(pl.multiple_of(d * cap, 8), cap)],
             dst_ref=lag_in.at[pl.ds(pl.multiple_of(slot * cap, 8), cap)],
-            send_sem=send_sem.at[2, d], recv_sem=recv_sem.at[2, slot], device_id=place(d), device_id_type=MESH,
+            send_sem=send_sem.at[PARTS + 1, d], recv_sem=recv_sem.at[PARTS + 1, slot], device_id=place(d), device_id_type=MESH,
         )
 
     def rec_copy(d, slot):
         return pltpu.make_async_remote_copy(
             src_ref=rec_out.at[pl.ds(pl.multiple_of(d * REC_DEV, 8), REC_DEV)],
             dst_ref=rec_in.at[pl.ds(pl.multiple_of(slot * REC_DEV, 8), REC_DEV)],
-            send_sem=send_sem.at[3, d], recv_sem=recv_sem.at[3, slot], device_id=place(d), device_id_type=MESH,
-        )
-
-    statics_row = statics_ref[...]
-    eye = iota((traces, traces), 0) == iota((traces, traces), 1)
-    amount = jnp.sum(jnp.where(eye, statics_row, 0), axis=1, keepdims=True) + MAX_SHIFT
-    step = 16
-    for first in range(0, traces, step):
-        row = jnp.concatenate([traces_ref[first : first + step, :], jnp.zeros((step, BLOCK), f32)], axis=1)
-        width = samples + BLOCK
-        here = amount[first : first + step]
-        row = pltpu.roll(row, width - MAX_SHIFT, 1)
-        for bit in range((2 * MAX_SHIFT).bit_length()):
-            row = jnp.where((here >> bit) & 1 == 1, pltpu.roll(row, 1 << bit, 1), row)
-        high, low = halves(row[:, :samples])
-        shifted[first : first + step, :] = high
-        shifted[traces + first : traces + first + step, :] = low
+            send_sem=send_sem.at[PARTS + 2, d], recv_sem=recv_sem.at[PARTS + 2, slot], device_id=place(d), device_id_type=MESH,
+        )
+
+    for load in loads[:5]:
+        load.wait()
 
     owner = owner_ref[...]
     member = iota((n, traces), 0) == owner
@@ -145,8 +159,6 @@
     target = owner * cap + rank
     put = onehot(iota((rows, traces), 0) == target)
     put_twice = jnp.concatenate([put, put], axis=1)
-    for first in range(0, samples, 3 * BLOCK):
-        outbox[:, first : first + 3 * BLOCK] = mm(put_twice, shifted[:, first : first + 3 * BLOCK])
 
     seat = iota((BLOCK, traces), 0)
     bins_here = jnp.where(member, (offset_ref[...] + 1).astype(f32), 0.0)
@@ -171,11 +183,40 @@
     def _(k):
         d = lax.rem(me + k, n)
         label_copy(d, me).start()
-        trace_copy(d, me).start()
-
+
+    label_in[me] = label_out[me]
     mine = pl.ds(pl.multiple_of(me * cap, 8), cap)
-    inbox[mine, :] = outbox[mine, :]
-    label_in[me] = label_out[me]
+
+    eye = iota((traces, traces), 0) == iota((traces, traces), 1)
+    amount = jnp.sum(jnp.where(eye, statics_ref[...], 0), axis=1, keepdims=True) + MAX_SHIFT
+    step = 16
+    width = part + 2 * BLOCK
+    loads[5].wait()
+    for c in range(PARTS):
+        low_end, high_end = c * part - BLOCK, (c + 1) * part + BLOCK
+        columns = slice(c * part, (c + 1) * part)
+        for first in range(0, traces, step):
+            row = traces_ref[first : first + step, max(low_end, 0) : min(high_end, samples)]
+            edge = jnp.zeros((step, BLOCK), f32)
+            if low_end < 0:
+                row = jnp.concatenate([edge, row], axis=1)
+            if high_end > samples:
+                row = jnp.concatenate([row, edge], axis=1)
+            here = amount[first : first + step]
+            row = pltpu.roll(row, width - MAX_SHIFT, 1)
+            for bit in range((2 * MAX_SHIFT).bit_length()):
+                row = jnp.where((here >> bit) & 1 == 1, pltpu.roll(row, 1 << bit, 1), row)
+            high, low = halves(row[:, BLOCK : BLOCK + part])
+            shifted[first : first + step, columns] = high
+            shifted[traces + first : traces + first + step, columns] = low
+        outbox[:, columns] = mm(put_twice, shifted[:, columns])
+
+        @pl.loop(1, n)
+        def _(k):
+            d = lax.rem(me + k, n)
+            trace_copy(c, d, me).start()
+
+        inbox[mine, columns] = outbox[mine, columns]
 
     own_shot = onehot(iota((SHOT_DEV, traces), 0) == lax.rem(shot_ref[...], SHOT_DEV))
     take = mm_nt(own_shot, put).astype(bf16)
@@ -184,7 +225,6 @@
     def _(k):
         d = lax.rem(me + (n - k), n)
         label_copy(d, d).wait_recv()
-        trace_copy(d, d).wait_recv()
 
     @pl.loop(0, n)
     def _(d):
@@ -208,36 +248,56 @@
     stack = onehot(iota((CMP_DEV, rows), 0) == bin_row)
     pick = onehot(iota((REC_DEV * n, rows), 0) == rec_row)
 
-    pilots = []
-    for j in range(blocks):
-        high, low = halves(inbox[:, j * BLOCK : (j + 1) * BLOCK])
-        pilots.append(mm(stack, high) + mm(stack, low))
-    pilots.append(jnp.zeros((CMP_DEV, BLOCK), f32))
-    moved = pltpu.roll(jnp.concatenate(pilots, axis=1), LAGS // 2, 1)
+    for load in loads[6:]:
+        load.wait()
     fwd_high, fwd_low = fwd_high_ref[...], fwd_low_ref[...]
-    for j in range(blocks + 1):
-        spectra[j] = mm3(moved[:, j * BLOCK : (j + 1) * BLOCK], fwd_high, fwd_low)
-
     lane = iota((CMP_DEV, BLOCK), 1)
     turn = (1 - 2 * (iota((CMP_DEV, 2 * BLOCK), 1) % 2)).astype(f32)
     corr[...] = jnp.zeros_like(corr)
-
-    @pl.loop(0, blocks)
-    def _(j):
+    half = LAGS // 2
+    before = jnp.zeros((CMP_DEV, half), f32)
+
+    def block_spectrum(pilot, before):
+        return mm3(jnp.concatenate([before, pilot[:, :half]], axis=1), fwd_high, fwd_low)
+
+    def add_block(j):
         window = spectra[j] + turn * spectra[j + 1]
         real, imag = window[:, :BLOCK], window[:, BLOCK:]
         wide = jnp.concatenate(
             [real, jnp.where(lane == 0, 0.0, imag), jnp.where(lane == 0, -imag, real)], axis=1
         )
         w = mm(gather_twice, jnp.concatenate(halves(wide), axis=0))
-        y = mm3(inbox[:, pl.ds(pl.multiple_of(j * BLOCK, BLOCK), BLOCK)], fwd_high, fwd_low)
+        y = mm3(inbox[:, pl.ds(j * BLOCK, BLOCK)], fwd_high, fwd_low)
         y_real, y_imag = y[:, :BLOCK], y[:, BLOCK:]
         w_real, w_imag, w_other = w[:, :BLOCK], w[:, BLOCK : 2 * BLOCK], w[:, 2 * BLOCK :]
         corr[:, :BLOCK] += y_real * w_real + y_imag * w_imag
         corr[:, BLOCK:] += y_real * w_imag - y_imag * w_other
 
+    for c in range(PARTS):
+
+        @pl.loop(1, n)
+        def _(k):
+            d = lax.rem(me + (n - k), n)
+            trace_copy(c, d, d).wait_recv()
+
+        for j in range(c * per_part, (c + 1) * per_part):
+            high, low = halves(inbox[:, j * BLOCK : (j + 1) * BLOCK])
+            pilot = mm(stack, high) + mm(stack, low)
+            spectra[j] = block_spectrum(pilot, before)
+            before = pilot[:, half:]
+            if j > 0:
+                add_block(j - 1)
+    spectra[blocks] = block_spectrum(jnp.zeros((CMP_DEV, BLOCK), f32), before)
+    add_block(blocks - 1)
+
     lagged = mm3(corr[...], inv_high_ref[...], inv_low_ref[...])
     lag_out[...] = lagged
+
+    @pl.loop(1, n)
+    def _(k):
+        d = lax.rem(me + k, n)
+        lag_copy(d, me).start()
+
     high, low = halves(lagged)
     rec_out[...] = mm(pick, high) + mm(pick, low)
 
@@ -245,7 +305,6 @@
     def _(k):
         d = lax.rem(me + k, n)
         rec_copy(d, me).start()
-        lag_copy(d, me).start()
 
     lag_in[mine, :] = lag_out[mine, :]
     mine_rec = pl.ds(pl.multiple_of(me * REC_DEV, 8), REC_DEV)
@@ -268,7 +327,8 @@
     def _(k):
         d = lax.rem(me + k, n)
         label_copy(d, me).wait_send()
-        trace_copy(d, me).wait_send()
+        for c in range(PARTS):
+            trace_copy(c, d, me).wait_send()
         rec_copy(d, me).wait_send()
         lag_copy(d, me).wait_send()
 
@@ -289,9 +349,12 @@
             jax.ShapeDtypeStruct((SHOT_DEV, LAGS), f32),
             jax.ShapeDtypeStruct((REC_DEV, LAGS), f32),
         ),
-        in_specs=[vmem] * 10,
+        in_specs=[pl.BlockSpec(memory_space=pl.ANY)] * 10,
         out_specs=(vmem, vmem),
-        scratch_shapes=[
+        scratch_shapes=[pltpu.VMEM((1, count), jnp.int32) for _ in range(5)]
+        + [pltpu.VMEM((count, samples), f32)]
+        + [pltpu.VMEM(t.shape, bf16) for t in tables]
+        + [
             pltpu.VMEM((2 * count, samples), bf16),
             pltpu.VMEM((rows, samples), f32),
             pltpu.VMEM((rows, samples), f32),
@@ -304,8 +367,9 @@
             pltpu.VMEM((rows, LAGS), f32),
             pltpu.VMEM((n * REC_DEV, LAGS), f32),
             pltpu.VMEM((n * REC_DEV, LAGS), f32),
-            pltpu.SemaphoreType.DMA((4, n)),
-            pltpu.SemaphoreType.DMA((4, n)),
+            pltpu.SemaphoreType.DMA((PARTS + 3, n)),
+            pltpu.SemaphoreType.DMA((PARTS + 3, n)),
+            pltpu.SemaphoreType.DMA((10,)),
         ],
         compiler_params=pltpu.CompilerParams(
             collective_id=0, has_side_effects=True, vmem_limit_bytes=48 * 1024 * 1024

time: 77.5 us -> 78.2 us (level)
  no operation moved by 1% of the time
where the time goes in v2:
time: 78.2 us; the launch traced here: 77.8 us
  Pallas kernels  70.7 us (90%)
  local copies, waits for them, and re-layouts  6.43 us (8%)
    pallas_call x1, Pallas kernels, local(): pl.pallas_call(functools.partial(kernel, n, n_cmp, cap), out_shape=(jax.S...  70.7 us
    unnamed x22, local copies, waits for them, and re-layouts  6.43 us

profile of v2, /device:TPU:0, one launch (start us, length us, event | category | flops | bytes accessed | tf_op | source)
XLA Modules:
  0.0 77.8 jit_solution(18097585623211318513)
XLA Ops:
  0.6 0.0 copy-start.8
  0.6 0.0 copy-start.9
  0.7 0.0 copy-start.5
  0.7 0.0 copy-start.6
  0.7 0.0 copy-start.7
  0.7 0.6 copy-done.8
  1.3 0.0 copy-done.9
  1.3 0.0 copy-done.5
  1.3 0.0 copy-done.6
  1.3 0.0 copy-done.7
  1.4 0.0 copy-start
  1.4 1.2 %copy-done = f32[128,1920]{1,0:T(8,128)S(1)} copy-done((f32[128,1920]{1,0:T(8,128)S(1)}, f32[128,1920]{1,0:T(8,128)}, u32[]{:S(2)}) %copy-start) | copy-done | bytes 983064
  2.6 0.0 copy-start.1
  2.6 0.8 %copy-done.1 = bf16[256,128]{1,0:T(8,128)(2,1)S(1)} copy-done((bf16[256,128]{1,0:T(8,128)(2,1)S(1)}, bf16[256,128]{1,0:T(8,128)(2,1)}, u32[]{:S(2)}) %copy-start.1) | copy-done | bytes 65560
  3.4 0.0 copy-start.2
  3.4 0.8 %copy-done.2 = bf16[256,128]{1,0:T(8,128)(2,1)S(1)} copy-done((bf16[256,128]{1,0:T(8,128)(2,1)S(1)}, bf16[256,128]{1,0:T(8,128)(2,1)}, u32[]{:S(2)}) %copy-start.2) | copy-done | bytes 65560
  4.2 0.0 copy-start.3
  4.2 0.8 %copy-done.3 = bf16[128,256]{1,0:T(8,128)(2,1)S(1)} copy-done((bf16[128,256]{1,0:T(8,128)(2,1)S(1)}, bf16[128,256]{1,0:T(8,128)(2,1)}, u32[]{:S(2)}) %copy-start.3) | copy-done | bytes 65560
  5.1 0.0 copy-start.4
  5.1 0.8 %copy-done.4 = bf16[128,256]{1,0:T(8,128)(2,1)S(1)} copy-done((bf16[128,256]{1,0:T(8,128)(2,1)S(1)}, bf16[128,256]{1,0:T(8,128)(2,1)}, u32[]{:S(2)}) %copy-start.4) | copy-done | bytes 65560
  5.9 70.7 %shard_map.113 = (f32[16,128]{1,0:T(8,128)S(1)}, f32[16,128]{1,0:T(8,128)S(1)}) custom-call(s32[1,128]{1,0:T(1,128)S(1)} %bitcast.5, s32[1,128]{1,0:T(1,128)S(1)} %bitcast.6, s32[1,128]{1,0:T(1,128)S(1)} %bitcast.7, s32[1,128]{1,0:T(1,128)S(1)} %bitcast.8, s32[1,128]{1,0:T(1,128)S(1)} %bitcast.9, f32[128,1920]{1,0:T(8,128)S(1)} %copy-done, ...), custom_call_target="tpu_custom_call" | custom-call | tf_op jit(solution)/shard_map/pallas_call | solution.py:346
  76.6 0.6 copy.14
  77.2 0.6 copy.15
Async XLA Ops:
  0.6 0.7 copy-start.8
  0.6 0.7 copy-start.9
  0.7 0.7 copy-start.5
  0.7 0.7 copy-start.6
  0.7 0.7 copy-start.7
  1.4 1.2 %copy-start = (f32[128,1920]{1,0:T(8,128)S(1)}, f32[128,1920]{1,0:T(8,128)}, u32[]{:S(2)}) copy-start(f32[128,1920]{1,0:T(8,128)} %traces_any.1) | copy-start | bytes 2949124
  2.6 0.8 %copy-start.1 = (bf16[256,128]{1,0:T(8,128)(2,1)S(1)}, bf16[256,128]{1,0:T(8,128)(2,1)}, u32[]{:S(2)}) copy-start(bf16[256,128]{1,0:T(8,128)(2,1)} %constant.11.clone.inv_low_any) | copy-start | bytes 196612
  3.4 0.8 %copy-start.2 = (bf16[256,128]{1,0:T(8,128)(2,1)S(1)}, bf16[256,128]{1,0:T(8,128)(2,1)}, u32[]{:S(2)}) copy-start(bf16[256,128]{1,0:T(8,128)(2,1)} %constant.10.clone.inv_high_any) | copy-start | bytes 196612
  4.2 0.8 %copy-start.3 = (bf16[128,256]{1,0:T(8,128)(2,1)S(1)}, bf16[128,256]{1,0:T(8,128)(2,1)}, u32[]{:S(2)}) copy-start(bf16[128,256]{1,0:T(8,128)(2,1)} %constant.9.clone.fwd_low_any) | copy-start | bytes 196612
  5.1 0.8 %copy-start.4 = (bf16[128,256]{1,0:T(8,128)(2,1)S(1)}, bf16[128,256]{1,0:T(8,128)(2,1)}, u32[]{:S(2)}) copy-start(bf16[128,256]{1,0:T(8,128)(2,1)} %constant.8.clone.fwd_high_any) | copy-start | bytes 196612

commit v3 on v2

--- a/solution.py
+++ b/solution.py
@@ -81,15 +81,21 @@
     source_ref, received_ref,
     owner_ref, offset_ref, shot_ref, receiver_ref, statics_ref, traces_ref,
     fwd_high_ref, fwd_low_ref, inv_high_ref, inv_low_ref,
-    shifted, outbox, inbox, label_rows, label_out, label_in, spectra, corr, lag_out, lag_in, rec_out, rec_in,
-    send_sem, recv_sem, load_sem,
+    shifted, outbox, inbox, label_rows, label_out, label_in, spectra, corr, lag_out, lag_in, rec_out, rec_side, rec_in,
+    send_sem, recv_sem, side_sem, load_sem,
 ):
     rows = n * cap
     traces, samples = traces_ref.shape
     blocks = samples // BLOCK
     part = samples // PARTS
     per_part = blocks // PARTS
-    me = lax.axis_index("shot") * n_cmp + lax.axis_index("cmp")
+    shot, cmp = lax.axis_index("shot"), lax.axis_index("cmp")
+    me = shot * n_cmp + cmp
+    pairs = n // n_cmp // 2
+    core = lax.rem(shot, 2)
+    team = n // 2
+    rank_in_team = shot // 2 * n_cmp + cmp
+    shot_rows = n_cmp * REC_DEV
 
     def place(d):
         return (d // n_cmp, lax.rem(d, n_cmp))
@@ -141,11 +147,24 @@
             send_sem=send_sem.at[PARTS + 1, d], recv_sem=recv_sem.at[PARTS + 1, slot], device_id=place(d), device_id_type=MESH,
         )
 
-    def rec_copy(d, slot):
+    def shot_block(i, c):
+        return pl.ds(pl.multiple_of((2 * i + c) * shot_rows, 8), shot_rows)
+
+    def side_copy(i):
+        return pltpu.make_async_remote_copy(
+            src_ref=rec_out.at[shot_block(i, 1 - core)],
+            dst_ref=rec_side.at[pl.ds(i * shot_rows, shot_rows)],
+            send_sem=side_sem.at[0, i], recv_sem=side_sem.at[1, i],
+            device_id=(shot + 1 - 2 * core, cmp), device_id_type=MESH,
+        )
+
+    def rec_copy(p, slot):
+        d = (2 * (p // n_cmp) + core) * n_cmp + lax.rem(p, n_cmp)
         return pltpu.make_async_remote_copy(
             src_ref=rec_out.at[pl.ds(pl.multiple_of(d * REC_DEV, 8), REC_DEV)],
             dst_ref=rec_in.at[pl.ds(pl.multiple_of(slot * REC_DEV, 8), REC_DEV)],
-            send_sem=send_sem.at[PARTS + 2, d], recv_sem=recv_sem.at[PARTS + 2, slot], device_id=place(d), device_id_type=MESH,
+            send_sem=send_sem.at[PARTS + 2, p], recv_sem=recv_sem.at[PARTS + 2, slot],
+            device_id=place(d), device_id_type=MESH,
         )
 
     for load in loads[:5]:
@@ -301,25 +320,36 @@
     high, low = halves(lagged)
     rec_out[...] = mm(pick, high) + mm(pick, low)
 
-    @pl.loop(1, n)
-    def _(k):
-        d = lax.rem(me + k, n)
-        rec_copy(d, me).start()
+    for i in range(pairs):
+        side_copy(i).start()
 
     lag_in[mine, :] = lag_out[mine, :]
-    mine_rec = pl.ds(pl.multiple_of(me * REC_DEV, 8), REC_DEV)
-    rec_in[mine_rec, :] = rec_out[mine_rec, :]
+    for i in range(pairs):
+        side_copy(i).wait_recv()
+        rec_out[shot_block(i, core), :] += rec_side[i * shot_rows : (i + 1) * shot_rows, :]
+
+    @pl.loop(1, team)
+    def _(k):
+        rec_copy(lax.rem(rank_in_team + k, team), rank_in_team).start()
+
+    own_rows = pl.ds(pl.multiple_of(rank_in_team * REC_DEV, 8), REC_DEV)
+    rec_in[own_rows, :] = rec_out[pl.ds(pl.multiple_of(me * REC_DEV, 8), REC_DEV), :]
 
     @pl.loop(1, n)
     def _(k):
         d = lax.rem(me + (n - k), n)
-        rec_copy(d, d).wait_recv()
         lag_copy(d, d).wait_recv()
 
     high, low = halves(lag_in[...])
     source_ref[...] = mm(take, high) + mm(take, low)
+
+    @pl.loop(1, team)
+    def _(k):
+        p = lax.rem(rank_in_team + (team - k), team)
+        rec_copy(p, p).wait_recv()
+
     total = rec_in[0:REC_DEV, :]
-    for d in range(1, n):
+    for d in range(1, team):
         total = total + rec_in[d * REC_DEV : (d + 1) * REC_DEV, :]
     received_ref[...] = total
 
@@ -329,8 +359,14 @@
         label_copy(d, me).wait_send()
         for c in range(PARTS):
             trace_copy(c, d, me).wait_send()
-        rec_copy(d, me).wait_send()
         lag_copy(d, me).wait_send()
+
+    for i in range(pairs):
+        side_copy(i).wait_send()
+
+    @pl.loop(1, team)
+    def _(k):
+        rec_copy(lax.rem(rank_in_team + k, team), rank_in_team).wait_send()
 
 
 def local(n, n_cmp, traces, statics, cmp_owner, cmp_offset, shot_id, receiver_id):
@@ -349,7 +385,7 @@
             jax.ShapeDtypeStruct((SHOT_DEV, LAGS), f32),
             jax.ShapeDtypeStruct((REC_DEV, LAGS), f32),
         ),
-        in_specs=[pl.BlockSpec(memory_space=pl.ANY)] * 10,
+        in_specs=[pl.BlockSpec(memory_space=pltpu.HBM)] * 10,
         out_specs=(vmem, vmem),
         scratch_shapes=[pltpu.VMEM((1, count), jnp.int32) for _ in range(5)]
         + [pltpu.VMEM((count, samples), f32)]
@@ -366,9 +402,11 @@
             pltpu.VMEM((rows, LAGS), f32),
             pltpu.VMEM((rows, LAGS), f32),
             pltpu.VMEM((n * REC_DEV, LAGS), f32),
-            pltpu.VMEM((n * REC_DEV, LAGS), f32),
+            pltpu.VMEM((n // 2 * REC_DEV, LAGS), f32),
+            pltpu.VMEM((n // 2 * REC_DEV, LAGS), f32),
             pltpu.SemaphoreType.DMA((PARTS + 3, n)),
             pltpu.SemaphoreType.DMA((PARTS + 3, n)),
+            pltpu.SemaphoreType.DMA((2, n // n_cmp // 2)),
             pltpu.SemaphoreType.DMA((10,)),
         ],
         compiler_params=pltpu.CompilerParams(

time: 78.2 us -> 75.4 us (0.964)
  Pallas kernels: 70.7 us -> 67.9 us
    pallas_call x1, Pallas kernels: 70.7 us -> 67.9 us  [local(): pl.pallas_call(functools.partial(kernel, n, n_cmp, cap), out_shape=(jax.S...]
where the time goes in v3:
time: 75.4 us; the launch traced here: 75 us
  Pallas kernels  67.9 us (90%)
  local copies, waits for them, and re-layouts  6.43 us (9%)
    pallas_call x1, Pallas kernels, local(): pl.pallas_call(functools.partial(kernel, n, n_cmp, cap), out_shape=(jax.S...  67.9 us
    unnamed x22, local copies, waits for them, and re-layouts  6.43 us

profile of v3, /device:TPU:0, one launch (start us, length us, event | category | flops | bytes accessed | tf_op | source)
XLA Modules:
  0.0 75.0 jit_solution(7476169114645993676)
XLA Ops:
  0.6 0.0 copy-start.8
  0.6 0.0 copy-start.9
  0.7 0.0 copy-start.5
  0.7 0.0 copy-start.6
  0.7 0.0 copy-start.7
  0.7 0.6 copy-done.8
  1.3 0.0 copy-done.9
  1.3 0.0 copy-done.5
  1.3 0.0 copy-done.6
  1.3 0.0 copy-done.7
  1.4 0.0 copy-start
  1.4 1.2 %copy-done = f32[128,1920]{1,0:T(8,128)S(1)} copy-done((f32[128,1920]{1,0:T(8,128)S(1)}, f32[128,1920]{1,0:T(8,128)}, u32[]{:S(2)}) %copy-start) | copy-done | bytes 983064
  2.6 0.0 copy-start.1
  2.6 0.8 %copy-done.1 = bf16[256,128]{1,0:T(8,128)(2,1)S(1)} copy-done((bf16[256,128]{1,0:T(8,128)(2,1)S(1)}, bf16[256,128]{1,0:T(8,128)(2,1)}, u32[]{:S(2)}) %copy-start.1) | copy-done | bytes 65560
  3.4 0.0 copy-start.2
  3.4 0.8 %copy-done.2 = bf16[256,128]{1,0:T(8,128)(2,1)S(1)} copy-done((bf16[256,128]{1,0:T(8,128)(2,1)S(1)}, bf16[256,128]{1,0:T(8,128)(2,1)}, u32[]{:S(2)}) %copy-start.2) | copy-done | bytes 65560
  4.2 0.0 copy-start.3
  4.2 0.8 %copy-done.3 = bf16[128,256]{1,0:T(8,128)(2,1)S(1)} copy-done((bf16[128,256]{1,0:T(8,128)(2,1)S(1)}, bf16[128,256]{1,0:T(8,128)(2,1)}, u32[]{:S(2)}) %copy-start.3) | copy-done | bytes 65560
  5.1 0.0 copy-start.4
  5.1 0.8 %copy-done.4 = bf16[128,256]{1,0:T(8,128)(2,1)S(1)} copy-done((bf16[128,256]{1,0:T(8,128)(2,1)S(1)}, bf16[128,256]{1,0:T(8,128)(2,1)}, u32[]{:S(2)}) %copy-start.4) | copy-done | bytes 65560
  5.9 67.9 %shard_map.113 = (f32[16,128]{1,0:T(8,128)S(1)}, f32[16,128]{1,0:T(8,128)S(1)}) custom-call(s32[1,128]{1,0:T(1,128)S(1)} %bitcast.5, s32[1,128]{1,0:T(1,128)S(1)} %bitcast.6, s32[1,128]{1,0:T(1,128)S(1)} %bitcast.7, s32[1,128]{1,0:T(1,128)S(1)} %bitcast.8, s32[1,128]{1,0:T(1,128)S(1)} %bitcast.9, f32[128,1920]{1,0:T(8,128)S(1)} %copy-done, ...), custom_call_target="tpu_custom_call" | custom-call | tf_op jit(solution)/shard_map/pallas_call | solution.py:382
  73.8 0.6 copy.14
  74.4 0.6 copy.15
Async XLA Ops:
  0.6 0.7 copy-start.8
  0.6 0.7 copy-start.9
  0.7 0.7 copy-start.5
  0.7 0.7 copy-start.6
  0.7 0.7 copy-start.7
  1.4 1.2 %copy-start = (f32[128,1920]{1,0:T(8,128)S(1)}, f32[128,1920]{1,0:T(8,128)}, u32[]{:S(2)}) copy-start(f32[128,1920]{1,0:T(8,128)} %traces_any.1) | copy-start | bytes 2949124
  2.6 0.8 %copy-start.1 = (bf16[256,128]{1,0:T(8,128)(2,1)S(1)}, bf16[256,128]{1,0:T(8,128)(2,1)}, u32[]{:S(2)}) copy-start(bf16[256,128]{1,0:T(8,128)(2,1)} %constant.11.clone.inv_low_any) | copy-start | bytes 196612
  3.4 0.8 %copy-start.2 = (bf16[256,128]{1,0:T(8,128)(2,1)S(1)}, bf16[256,128]{1,0:T(8,128)(2,1)}, u32[]{:S(2)}) copy-start(bf16[256,128]{1,0:T(8,128)(2,1)} %constant.10.clone.inv_high_any) | copy-start | bytes 196612
  4.2 0.8 %copy-start.3 = (bf16[128,256]{1,0:T(8,128)(2,1)S(1)}, bf16[128,256]{1,0:T(8,128)(2,1)}, u32[]{:S(2)}) copy-start(bf16[128,256]{1,0:T(8,128)(2,1)} %constant.9.clone.fwd_low_any) | copy-start | bytes 196612
  5.1 0.8 %copy-start.4 = (bf16[128,256]{1,0:T(8,128)(2,1)S(1)}, bf16[128,256]{1,0:T(8,128)(2,1)}, u32[]{:S(2)}) copy-start(bf16[128,256]{1,0:T(8,128)(2,1)} %constant.8.clone.fwd_high_any) | copy-start | bytes 196612

commit v4 on v3

--- a/solution.py
+++ b/solution.py
@@ -15,7 +15,9 @@
 SHOT_DEV = 16
 REC_DEV = 16
 BLOCK = 128
-PARTS = 3
+SIZES = (6, 6, 3)
+PARTS = len(SIZES)
+ENDS = tuple(sum(SIZES[:i]) for i in range(PARTS + 1))
 STACK_SCALE = 0.125
 
 f32 = jnp.float32
@@ -87,8 +89,6 @@
     rows = n * cap
     traces, samples = traces_ref.shape
     blocks = samples // BLOCK
-    part = samples // PARTS
-    per_part = blocks // PARTS
     shot, cmp = lax.axis_index("shot"), lax.axis_index("cmp")
     me = shot * n_cmp + cmp
     pairs = n // n_cmp // 2
@@ -127,7 +127,7 @@
         pl.semaphore_signal(barrier, inc=1, device_id=place(lax.rem(me + k, n)), device_id_type=MESH)
 
     def trace_copy(c, d, slot):
-        columns = pl.ds(c * part, part)
+        columns = pl.ds(ENDS[c] * BLOCK, SIZES[c] * BLOCK)
         return pltpu.make_async_remote_copy(
             src_ref=outbox.at[pl.ds(pl.multiple_of(d * cap, 8), cap), columns],
             dst_ref=inbox.at[pl.ds(pl.multiple_of(slot * cap, 8), cap), columns],
@@ -209,11 +209,12 @@
     eye = iota((traces, traces), 0) == iota((traces, traces), 1)
     amount = jnp.sum(jnp.where(eye, statics_ref[...], 0), axis=1, keepdims=True) + MAX_SHIFT
     step = 16
-    width = part + 2 * BLOCK
     loads[5].wait()
     for c in range(PARTS):
-        low_end, high_end = c * part - BLOCK, (c + 1) * part + BLOCK
-        columns = slice(c * part, (c + 1) * part)
+        part = SIZES[c] * BLOCK
+        width = part + 2 * BLOCK
+        low_end, high_end = (ENDS[c] - 1) * BLOCK, (ENDS[c + 1] + 1) * BLOCK
+        columns = slice(ENDS[c] * BLOCK, ENDS[c + 1] * BLOCK)
         for first in range(0, traces, step):
             row = traces_ref[first : first + step, max(low_end, 0) : min(high_end, samples)]
             edge = jnp.zeros((step, BLOCK), f32)
@@ -299,7 +300,7 @@
             d = lax.rem(me + (n - k), n)
             trace_copy(c, d, d).wait_recv()
 
-        for j in range(c * per_part, (c + 1) * per_part):
+        for j in range(ENDS[c], ENDS[c + 1]):
             high, low = halves(inbox[:, j * BLOCK : (j + 1) * BLOCK])
             pilot = mm(stack, high) + mm(stack, low)
             spectra[j] = block_spectrum(pilot, before)

time: 75.4 us -> 74.8 us (level)
  no operation moved by 1% of the time
where the time goes in v4:
time: 74.8 us; the launch traced here: 74.5 us
  Pallas kernels  67.4 us (90%)
  local copies, waits for them, and re-layouts  6.43 us (9%)
    pallas_call x1, Pallas kernels, local(): pl.pallas_call(functools.partial(kernel, n, n_cmp, cap), out_shape=(jax.S...  67.4 us
    unnamed x22, local copies, waits for them, and re-layouts  6.43 us

profile of v4, /device:TPU:0, one launch (start us, length us, event | category | flops | bytes accessed | tf_op | source)
XLA Modules:
  0.0 74.5 jit_solution(4857073286010268386)
XLA Ops:
  0.6 0.0 copy-start.8
  0.6 0.0 copy-start.9
  0.7 0.0 copy-start.5
  0.7 0.0 copy-start.6
  0.7 0.0 copy-start.7
  0.7 0.6 copy-done.8
  1.3 0.0 copy-done.9
  1.3 0.0 copy-done.5
  1.3 0.0 copy-done.6
  1.3 0.0 copy-done.7
  1.4 0.0 copy-start
  1.4 1.2 %copy-done = f32[128,1920]{1,0:T(8,128)S(1)} copy-done((f32[128,1920]{1,0:T(8,128)S(1)}, f32[128,1920]{1,0:T(8,128)}, u32[]{:S(2)}) %copy-start) | copy-done | bytes 983064
  2.6 0.0 copy-start.1
  2.6 0.8 %copy-done.1 = bf16[256,128]{1,0:T(8,128)(2,1)S(1)} copy-done((bf16[256,128]{1,0:T(8,128)(2,1)S(1)}, bf16[256,128]{1,0:T(8,128)(2,1)}, u32[]{:S(2)}) %copy-start.1) | copy-done | bytes 65560
  3.4 0.0 copy-start.2
  3.4 0.8 %copy-done.2 = bf16[256,128]{1,0:T(8,128)(2,1)S(1)} copy-done((bf16[256,128]{1,0:T(8,128)(2,1)S(1)}, bf16[256,128]{1,0:T(8,128)(2,1)}, u32[]{:S(2)}) %copy-start.2) | copy-done | bytes 65560
  4.2 0.0 copy-start.3
  4.2 0.8 %copy-done.3 = bf16[128,256]{1,0:T(8,128)(2,1)S(1)} copy-done((bf16[128,256]{1,0:T(8,128)(2,1)S(1)}, bf16[128,256]{1,0:T(8,128)(2,1)}, u32[]{:S(2)}) %copy-start.3) | copy-done | bytes 65560
  5.1 0.0 copy-start.4
  5.1 0.8 %copy-done.4 = bf16[128,256]{1,0:T(8,128)(2,1)S(1)} copy-done((bf16[128,256]{1,0:T(8,128)(2,1)S(1)}, bf16[128,256]{1,0:T(8,128)(2,1)}, u32[]{:S(2)}) %copy-start.4) | copy-done | bytes 65560
  5.9 67.4 %shard_map.113 = (f32[16,128]{1,0:T(8,128)S(1)}, f32[16,128]{1,0:T(8,128)S(1)}) custom-call(s32[1,128]{1,0:T(1,128)S(1)} %bitcast.5, s32[1,128]{1,0:T(1,128)S(1)} %bitcast.6, s32[1,128]{1,0:T(1,128)S(1)} %bitcast.7, s32[1,128]{1,0:T(1,128)S(1)} %bitcast.8, s32[1,128]{1,0:T(1,128)S(1)} %bitcast.9, f32[128,1920]{1,0:T(8,128)S(1)} %copy-done, ...), custom_call_target="tpu_custom_call" | custom-call | tf_op jit(solution)/shard_map/pallas_call | solution.py:383
  73.3 0.6 copy.14
  73.9 0.6 copy.15
Async XLA Ops:
  0.6 0.7 copy-start.8
  0.6 0.7 copy-start.9
  0.7 0.7 copy-start.5
  0.7 0.7 copy-start.6
  0.7 0.7 copy-start.7
  1.4 1.2 %copy-start = (f32[128,1920]{1,0:T(8,128)S(1)}, f32[128,1920]{1,0:T(8,128)}, u32[]{:S(2)}) copy-start(f32[128,1920]{1,0:T(8,128)} %traces_any.1) | copy-start | bytes 2949124
  2.6 0.8 %copy-start.1 = (bf16[256,128]{1,0:T(8,128)(2,1)S(1)}, bf16[256,128]{1,0:T(8,128)(2,1)}, u32[]{:S(2)}) copy-start(bf16[256,128]{1,0:T(8,128)(2,1)} %constant.11.clone.inv_low_any) | copy-start | bytes 196612
  3.4 0.8 %copy-start.2 = (bf16[256,128]{1,0:T(8,128)(2,1)S(1)}, bf16[256,128]{1,0:T(8,128)(2,1)}, u32[]{:S(2)}) copy-start(bf16[256,128]{1,0:T(8,128)(2,1)} %constant.10.clone.inv_high_any) | copy-start | bytes 196612
  4.2 0.8 %copy-start.3 = (bf16[128,256]{1,0:T(8,128)(2,1)S(1)}, bf16[128,256]{1,0:T(8,128)(2,1)}, u32[]{:S(2)}) copy-start(bf16[128,256]{1,0:T(8,128)(2,1)} %constant.9.clone.fwd_low_any) | copy-start | bytes 196612
  5.1 0.8 %copy-start.4 = (bf16[128,256]{1,0:T(8,128)(2,1)S(1)}, bf16[128,256]{1,0:T(8,128)(2,1)}, u32[]{:S(2)}) copy-start(bf16[128,256]{1,0:T(8,128)(2,1)} %constant.8.clone.fwd_high_any) | copy-start | bytes 196612
